TPU v7x, 1024 devices: a whole 8x8x8 slice. The times are simulated.
1024 devices in a mesh: rep: 32 (over y, x_hi), exp: 32 (over x_lo, z, core).
Axes of the slice: x: 8 (x_hi: 4, x_lo: 2; x = x_hi * 2 + x_lo), y: 8, z: 8, core: 2. Of those that a mesh axis runs over, the one named last changes fastest.
Arguments:
- cotangent: bfloat16 [131072, 4096], P(('rep', 'exp')), may hold values from -2.5 to 2.5
- routes: int32 [131072, 1], P(('rep', 'exp')), may hold values from 0 to 31; in each aligned block of 128 rows (0 to 127, 128 to 255, ...) at most 6 rows name the same one
- gate_weight: float32 [131072, 1], P(('rep', 'exp')), may hold values from 0.1 to 1
- down_weight: bfloat16 [32, 4096, 768], P('exp'), may hold values from -0.21875 to 0.21875
- saved_pre: bfloat16 [32, 32, 192, 1536], P('rep', 'exp'), may hold values from -6 to 6
Outputs:
- weight_grad: float32 [32, 4096, 768], P('exp', 'rep')
- input_grads: bfloat16 [32, 32, 192, 1536], P('rep', 'exp')
- token_grad: float32 [131072, 1], P(('rep', 'exp'))
Inputs may be any that keep to these rules, and one draw needn't show every extreme that they name: `routes`: the rows of one device name each expert at most 6 times; in every draw some device names some expert exactly 6 times.
All inputs are finite; a program needn't handle non-finite values.
Results may differ from a plain program's by a relative error of at most 0.019.
Values may be sent and summed in bfloat16 or wider, within the bound.
A program may use at most 64 MiB of HBM per device.

v0:
```python
import jax
import jax.numpy as jnp
from jax import lax
from jax.sharding import PartitionSpec as P


def shards(cotangent, routes, gate_weight, down_weight, saved_pre):
    peers = lax.axis_size("exp")
    rows_all = saved_pre.shape[2]
    capacity = rows_all // peers
    width = down_weight.shape[2]
    expert_ids = routes[:, 0]
    experts = lax.broadcasted_iota(jnp.int32, (1, peers), 1)
    one_hot = (expert_ids[:, None] == experts).astype(jnp.int32)
    earlier = jnp.cumsum(one_hot, axis=0) - one_hot
    position = jnp.sum(earlier * one_hot, axis=1)
    slot_ids = expert_ids * capacity + position
    slot_index = lax.broadcasted_iota(jnp.int32, (rows_all, 1), 0)
    placement = slot_index == slot_ids[None, :]
    outgoing = jnp.dot(
        placement.astype(jnp.bfloat16), cotangent, preferred_element_type=jnp.float32
    ).astype(jnp.bfloat16)
    send_weight = jnp.sum(jnp.where(placement, gate_weight[:, 0][None, :], 0.0), axis=1).astype(
        jnp.bfloat16
    )
    arrived, arrived_weight = (
        lax.all_to_all(
            outgoing.reshape(peers, capacity, -1), "exp", split_axis=0, concat_axis=0, tiled=True
        ),
        lax.all_to_all(
            send_weight.reshape(peers, capacity), "exp", split_axis=0, concat_axis=0, tiled=True
        ),
    )
    received = arrived.reshape(rows_all, -1)
    scale_col = arrived_weight.reshape(rows_all, 1).astype(jnp.float32)
    pulled = jnp.dot(received, down_weight[0], preferred_element_type=jnp.float32)
    saved_pair = saved_pre[0, 0].astype(jnp.float32)
    gate_pre = saved_pair[:, :width]
    up_pre = saved_pair[:, width:]
    sigmoid_gate = jax.nn.sigmoid(gate_pre)
    silu_gate = gate_pre * sigmoid_gate
    hidden = silu_gate * up_pre
    router = jnp.sum(pulled * hidden, axis=1)
    returned_grad = lax.all_to_all(
        router.reshape(peers, capacity), "exp", split_axis=0, concat_axis=0, tiled=True
    )
    token_grad = jnp.sum(jnp.where(placement, returned_grad.reshape(rows_all, 1), 0.0), axis=0)[
        :, None
    ]
    hidden_grad = scale_col * pulled
    gate_grad = hidden_grad * up_pre * sigmoid_gate * (1.0 + gate_pre * (1.0 - sigmoid_gate))
    up_grad = hidden_grad * silu_gate
    pair_grads = jnp.concatenate([gate_grad, up_grad], axis=1).astype(jnp.bfloat16)
    scaled = (scale_col * hidden).astype(jnp.bfloat16)
    partial_value = lax.dot_general(
        received, scaled, (((0,), (0,)), ((), ())), preferred_element_type=jnp.float32
    )
    grad_share = lax.psum_scatter(
        partial_value.astype(jnp.bfloat16), "rep", scatter_dimension=0, tiled=True
    ).astype(jnp.float32)
    return (grad_share[None], pair_grads.reshape(1, 1, rows_all, 2 * width), token_grad)


def solution(mesh):
    in_specs = (
        P(("rep", "exp"), None),
        P(("rep", "exp"), None),
        P(("rep", "exp"), None),
        P("exp", None, None),
        P("rep", "exp", None, None),
    )
    out_specs = (P("exp", "rep", None), P("rep", "exp", None, None), P(("rep", "exp"), None))
    return jax.shard_map(shards, mesh=mesh, in_specs=in_specs, out_specs=out_specs, check_vma=False)
```

profile of v0, /device:TPU:1, one launch (start us, length us, event | category | flops | bytes accessed | tf_op | source)
XLA Modules:
  0.0 365.8 jit_solution(10894881555569444966)
XLA Ops:
  7.2 0.0 copy-start
  7.2 0.8 fusion.6
  8.0 0.2 reduce_window_sum.11
  8.2 0.8 select_reduce_fusion.2
  9.0 0.7 multiply_add_fusion
  9.7 0.0 copy-done
  9.7 0.6 convolution_convert_fusion.1
  10.3 1.6 reshape.88
  11.9 19.3 %all-to-all-start = ((bf16[32,6,4096]{2,1,0:T(8,128)(2,1)}), bf16[32,6,4096]{2,1,0:T(8,128)(2,1)S(1)}, u32[]{:S(2)}, u32[]{:S(2)}) async-start(bf16[32,6,4096]{2,1,0:T(8,128)(2,1)} %reshape.88), calls=%async_computation | async-start | bytes 4194304 | tf_op jit(solution)/shard_map/all_to_all | solution.py:27
  31.2 0.0 reduce-scatter.2.cloned.1.call-start
  31.2 2.2 bitcast_convert_fusion
  33.4 49.6 %all-to-all-done = bf16[32,6,4096]{2,1,0:T(8,128)(2,1)S(1)} async-done(((bf16[32,6,4096]{2,1,0:T(8,128)(2,1)}), bf16[32,6,4096]{2,1,0:T(8,128)(2,1)S(1)}, u32[]{:S(2)}, u32[]{:S(2)}) %all-to-all-start) | async-done | bytes 1572896 | tf_op jit(solution)/shard_map/all_to_all | solution.py:27
  83.0 1.4 reshape.89
  84.5 0.0 copy-start.2
  84.5 0.0 copy-start.1
  84.5 5.1 %multiply_reduce_fusion = (f32[192]{0:T(256)S(1)}, f32[192,768]{1,0:T(8,128)S(1)}) fusion(f32[192,1536]{1,0:T(8,128)} %bitcast_convert_fusion, bf16[192,4096]{1,0:T(8,128)(2,1)} %reshape.89, bf16[1,4096,768]{2,1,0:T(8,128)(2,1)} %param.8), kind=kOutput, calls=%fused_computation.6 | convolution fusion | flops 1208991488 | bytes 9634560 | tf_op jit(solution)/shard_map/dot_general | solution.py:36
  89.5 0.1 all_to_all.15
  89.7 14.8 %all_to_all.20 = f32[32,1,6]{2,1,0:T(1,128)S(1)} all-to-all(f32[32,1,6]{2,1,0:T(1,128)S(1)} %bitcast.23), channel_id=1, replica_groups=mesh['rep'=32,'exp'=32] {'exp'}, dimensions={0} | all-to-all | bytes 1536 | tf_op jit(solution)/shard_map/all_to_all | solution.py:44
  104.5 0.5 broadcast.30
  105.0 0.7 reduce.7
  105.7 0.1 broadcast_in_dim.41
  105.8 0.0 copy-done.2
  105.8 0.6 select_reduce_fusion
  106.4 0.1 convert_element_type.65
  106.5 11.3 %all_to_all.21 = bf16[32,1,6]{2,1,0:T(2,128)(2,1)S(1)} all-to-all(bf16[32,1,6]{2,1,0:T(2,128)(2,1)S(1)} %convert_element_type.65), channel_id=1, replica_groups=mesh['rep'=32,'exp'=32] {'exp'}, dimensions={0} | all-to-all | bytes 768 | tf_op jit(solution)/shard_map/all_to_all | solution.py:30
  117.8 0.1 convert_reduce_fusion
  117.9 0.1 reshape.90
  118.0 0.0 copy-done.1
  118.0 6.0 %convolution_convert_fusion = bf16[4096,768]{1,0:T(8,128)(2,1)} fusion(bf16[192,4096]{1,0:T(8,128)(2,1)} %reshape.89, f32[192]{0:T(256)S(1)} %reshape.90, f32[192,1536]{1,0:T(8,128)S(1)} %copy-done.1), kind=kOutput, calls=%fused_computation | convolution fusion | flops 1212137472 | bytes 9044736 | tf_op jit(solution)/shard_map/dot_general | solution.py:55
  124.0 0.0 reduce-scatter.2.cloned.1.call-update
  124.0 0.3 fusion.5
  124.3 0.9 pad_maximum_fusion
  125.2 232.1 %reduce-scatter.2.cloned.1.call-done = bf16[128,768]{1,0:T(8,128)(2,1)} async-done(((bf16[4096,768]{1,0:T(8,128)(2,1)}), bf16[128,768]{1,0:T(8,128)(2,1)}) %reduce-scatter.2.cloned.1.call-update) | async-done | bytes 196624 | tf_op jit(solution)/shard_map/reduce_scatter | solution.py:58
  357.3 1.7 bitcast_convert_fusion.1
Async XLA Ops:
  7.2 2.5 copy-start
  11.9 71.2 %all-to-all-start = ((bf16[32,6,4096]{2,1,0:T(8,128)(2,1)}), bf16[32,6,4096]{2,1,0:T(8,128)(2,1)S(1)}, u32[]{:S(2)}, u32[]{:S(2)}) async-start(bf16[32,6,4096]{2,1,0:T(8,128)(2,1)} %reshape.88), calls=%async_computation | async-start | bytes 4194304 | tf_op jit(solution)/shard_map/all_to_all | solution.py:27
  31.2 326.1 %reduce-scatter.2.cloned.1.call-start = ((), (), s32[]{:S(2)}) async-start(), calls=%async_computation.4 | async-start | bytes 6488064 | tf_op jit(solution)/shard_map/reduce_scatter | solution.py:58
  84.5 21.3 %copy-start.2 = (f32[128,1]{0,1:T(1,128)S(1)}, f32[128,1]{0,1:T(1,128)}, u32[]{:S(2)}) copy-start(f32[128,1]{0,1:T(1,128)} %param.7) | copy-start | bytes 1540
  84.5 33.5 %copy-start.1 = (f32[192,1536]{1,0:T(8,128)S(1)}, f32[192,1536]{1,0:T(8,128)}, u32[]{:S(2)}) copy-start(f32[192,1536]{1,0:T(8,128)} %bitcast_convert_fusion) | copy-start | bytes 3538948
Sparse Core Ops, SparseCore 0:
  124.1 233.1 reduce-scatter.1
where the time goes:
time: 369 us; the launch traced here: 366 us
  waiting for transfers between devices  282 us (76%)
  blocking collectives  26.1 us (7%)
  starting transfers between devices  19.3 us (5%)
  between operations  14.1 us (4%)
  matrix products  11.6 us (3%)
  other arithmetic  8.96 us (2%)
  local copies, waits for them, and re-layouts  3.98 us (1%)
    reduce_scatter x1, waiting for transfers between devices, shards(): lax.psum_scatter(partial_value.astype(jnp.bfloat16), 'rep', scatter_dimen...  232 us
    all_to_all x1, waiting for transfers between devices, shards(): lax.all_to_all(outgoing.reshape(peers, capacity, -1), 'exp', split_axis=0...  49.6 us
    all_to_all x1, starting transfers between devices, shards(): lax.all_to_all(outgoing.reshape(peers, capacity, -1), 'exp', split_axis=0...  19.3 us
    all_to_all x1, blocking collectives, shards(): lax.all_to_all(router.reshape(peers, capacity), 'exp', split_axis=0, conc...  14.8 us
    all_to_all x1, blocking collectives, shards(): lax.all_to_all(send_weight.reshape(peers, capacity), 'exp', split_axis=0,...  11.3 us
  transfers between devices with their start and end apart: 2, of which 2 were waited for; matrix products, arithmetic and copies ran while one was open for 1% of the time, Pallas kernels for 0%

commit v1 on v0

v1 whole, which is shorter than its diff:
```python
import functools

import jax
import jax.numpy as jnp
from jax import lax
from jax.experimental import pallas as pl
from jax.experimental.pallas import tpu as pltpu
from jax.sharding import PartitionSpec as P

MESH = pl.DeviceIdType.MESH
BF = jnp.bfloat16
F32 = jnp.float32
CAP = 6
GROUP = 8
SUBS = 2


def dot(a, b, lhs=1, **kw):
    return lax.dot_general(a, b, (((lhs,), (0,)), ((), ())), preferred_element_type=F32, **kw)


def iota(shape, dim):
    return lax.broadcasted_iota(jnp.int32, shape, dim).astype(F32)


def kernel(
    ny, nx, peers,
    cot, routes, gate, weight_hbm, saved,
    grad_out, pair_out, token_out,
    weight, send, recv, arrived, place6, place8, swap, select,
    gate_send, gate_recv, router_send, router_recv,
    hidden, scale, scaled, pulled, ring_send, ring_recv, chunk, x_send, x_recv,
    weight_sem, send_sem, recv_sem, gate_ssem, gate_rsem, router_ssem, router_rsem,
    ring_ssem, ring_rsem, x_ssem, x_rsem,
):
    tokens = cot.shape[0]
    slots = peers * CAP
    groups = peers // GROUP
    width = weight.shape[1]
    half = cot.shape[1] // ny // 2
    steps = ny // 2
    rows = GROUP * CAP
    block = GROUP * rows
    msg = GROUP * CAP
    lanes = half // 2
    sub_w = width // SUBS
    out_rows = 2 * half // nx
    rep, me = lax.axis_index("rep"), lax.axis_index("exp")
    y, xh = rep // nx, rep % nx
    right = ((y + 1) % ny) * nx + xh
    left = ((y + ny - 1) % ny) * nx + xh

    weight_copy = pltpu.make_async_copy(weight_hbm, weight, weight_sem)
    weight_copy.start()

    barrier = pltpu.get_barrier_semaphore()

    @pl.loop(1, peers)
    def _(i):
        pl.semaphore_signal(
            barrier, inc=1, device_id=(rep, (me + i) % peers), device_id_type=MESH
        )

    for other in (left, right):
        pl.semaphore_signal(barrier, inc=1, device_id=(other, me), device_id_type=MESH)
    for i in range(1, nx):
        pl.semaphore_signal(
            barrier, inc=1, device_id=(y * nx + (xh + i) % nx, me), device_id_type=MESH
        )

    def column(which, k):
        at = (y + ny - 1 - k) % ny if which == 0 else (y + 1 + k) % ny
        return pl.multiple_of((at * 2 + which) * half, half)

    ids = routes[...].astype(F32)
    one_hot = ids == iota((tokens, peers), 1)
    below = (iota((tokens, tokens), 0) > iota((tokens, tokens), 1)).astype(F32).astype(BF)
    earlier = dot(below, one_hot.astype(F32).astype(BF))
    position = jnp.sum(jnp.where(one_hot, earlier, 0.0), axis=1, keepdims=True)
    place6[...] = (ids * CAP + position == iota((tokens, slots), 1)).astype(F32).astype(BF)
    place8[...] = (ids * 8 + position == iota((tokens, peers * 8), 1)).astype(F32)
    gate_b = jnp.broadcast_to(gate[...].astype(BF), (tokens, 128))
    gate_send[...] = dot(place8[...].astype(BF), gate_b, 0)

    r = iota((block, 1), 0)
    a = jnp.floor((r + 0.5) * (1.0 / rows))
    ab = jnp.floor((r + 0.5) * (1.0 / CAP))
    source = (ab - GROUP * a) * rows + a * CAP + (r - CAP * ab)
    swap[...] = (source == iota((block, block), 1)).astype(F32).astype(BF)
    r = iota((slots, 1), 0)
    spread = r + (8 - CAP) * jnp.floor((r + 0.5) * (1.0 / CAP))
    select[...] = (spread == iota((slots, peers * 8), 1)).astype(F32)

    def build(d):
        part = jnp.concatenate(
            [cot[:, pl.ds(column(w, 2 * d + i), half)] for w in range(2) for i in range(2)], axis=1
        )
        placed = dot(place6[...], part, 0).astype(BF)
        stacked = jnp.concatenate(
            [
                jnp.concatenate(
                    [
                        placed[g * rows : (g + 1) * rows, c * lanes : (c + 1) * lanes]
                        for c in range(GROUP)
                    ],
                    axis=0,
                )
                for g in range(groups)
            ],
            axis=1,
        )
        out = dot(swap[...], stacked).astype(BF)
        for g in range(groups):
            send[d, g * block : (g + 1) * block, :] = out[:, g * lanes : (g + 1) * lanes]

    def gate_copy(peer):
        return pltpu.make_async_remote_copy(
            src_ref=gate_send.at[pl.ds(pl.multiple_of(peer * 8, 8), 8)],
            dst_ref=gate_recv.at[pl.ds(pl.multiple_of(me * 8, 8), 8)],
            send_sem=gate_ssem, recv_sem=gate_rsem,
            device_id=(rep, peer), device_id_type=MESH,
        )

    def router_copy(peer):
        return pltpu.make_async_remote_copy(
            src_ref=router_send.at[pl.ds(pl.multiple_of(peer * 8, 8), 8)],
            dst_ref=router_recv.at[pl.ds(pl.multiple_of(me * 8, 8), 8)],
            send_sem=router_ssem, recv_sem=router_rsem,
            device_id=(rep, peer), device_id_type=MESH,
        )

    def row_copy(d, peer):
        return pltpu.make_async_remote_copy(
            src_ref=send.at[d, pl.ds(pl.multiple_of(peer * msg, msg), msg)],
            dst_ref=recv.at[d, pl.ds(pl.multiple_of(me * msg, msg), msg)],
            send_sem=send_sem.at[d], recv_sem=recv_sem.at[d],
            device_id=(rep, peer), device_id_type=MESH,
        )

    def wait_all(buffer, size, sem):
        part = buffer.at[pl.ds(0, (peers - 1) * size)]
        pltpu.make_async_copy(part, part, sem).wait()

    build(0)
    pl.semaphore_wait(barrier, peers - 1 + 2 + nx - 1)

    @pl.loop(1, peers)
    def _(i):
        gate_copy((me + i) % peers).start()

    @pl.loop(0, steps)
    def _(d):
        @pl.when(d > 0)
        def _():
            build(d)

        @pl.loop(1, peers)
        def _(i):
            row_copy(d, (me + i) % peers).start()

        mine = pl.ds(pl.multiple_of(me * msg, msg), msg)
        recv[d, mine, :] = send[d, mine, :]

    mine8 = pl.ds(pl.multiple_of(me * 8, 8), 8)
    gate_recv[mine8, :] = gate_send[mine8, :]

    g = saved[:, :width].astype(F32)
    u = saved[:, width:].astype(F32)
    hidden[...] = g * jax.nn.sigmoid(g) * u
    ring_recv[:, 0] = jnp.zeros(ring_recv.shape[:1] + ring_recv.shape[2:], BF)
    pulled[...] = jnp.zeros_like(pulled)

    wait_all(gate_recv, 8, gate_rsem)
    scale[...] = dot(select[...].astype(BF), gate_recv[...].astype(BF))[:, :1]
    scaled[...] = (scale[...] * hidden[...]).astype(BF)
    weight_copy.wait()

    def ring_copy(which, k, s):
        return pltpu.make_async_remote_copy(
            src_ref=ring_send.at[which, k, s],
            dst_ref=ring_recv.at[which, k + 1, s],
            send_sem=ring_ssem.at[which, k, s], recv_sem=ring_rsem.at[which, k, s],
            device_id=((left if which else right), me), device_id_type=MESH,
        )

    def term(d, i, which, s):
        at = (2 * which + i) * half
        return dot(arrived[d, :, at : at + half], scaled[:, s * sub_w : (s + 1) * sub_w], 0)

    def ring_step(d, i):
        k = 2 * d + i
        for s in range(SUBS):
            for which in range(2):
                own = term(d, i, which, s)
                if i == 1:
                    ring_copy(which, k - 1, s).wait_recv()
                else:

                    @pl.when(k > 0)
                    def _():
                        ring_copy(which, k - 1, s).wait_recv()

                ring_send[which, k, s] = (own + ring_recv[which, k, s].astype(F32)).astype(BF)
                ring_copy(which, k, s).start()

    @pl.loop(0, steps)
    def _(d):
        wait_all(recv.at[d], msg, recv_sem.at[d])
        stacked = jnp.concatenate(
            [recv[d, g * block : (g + 1) * block, :] for g in range(groups)], axis=1
        )
        out = dot(swap[...], stacked).astype(BF)
        for g in range(groups):
            for c in range(GROUP):
                arrived[d, g * rows : (g + 1) * rows, c * lanes : (c + 1) * lanes] = out[
                    c * rows : (c + 1) * rows, g * lanes : (g + 1) * lanes
                ]
        ring_step(d, 0)
        total = pulled[...]
        for w in range(2):
            for i in range(2):
                at = (2 * w + i) * half
                total = total + dot(
                    arrived[d, :, at : at + half], weight[pl.ds(column(w, 2 * d + i), half), :]
                )
        pulled[...] = total

        @pl.when(d < steps - 1)
        def _():
            ring_step(d, 1)

    router = jnp.sum(pulled[...] * hidden[...], axis=1, keepdims=True)
    router_send[...] = dot(
        select[...], jnp.broadcast_to(router, (slots, 128)), 0, precision=lax.Precision.HIGHEST
    )

    @pl.loop(1, peers)
    def _(i):
        router_copy((me + i) % peers).start()

    router_recv[mine8, :] = router_send[mine8, :]
    g = saved[:, :width].astype(F32)
    u = saved[:, width:].astype(F32)
    sg = jax.nn.sigmoid(g)
    dh = scale[...] * pulled[...]
    pair_out[:, :width] = (dh * u * sg * (1.0 + g * (1.0 - sg))).astype(BF)
    pair_out[:, width:] = (dh * g * sg).astype(BF)

    for s in range(SUBS):
        for which in range(2):
            own = term(steps - 1, 1, which, s)
            ring_copy(which, ny - 2, s).wait_recv()
            chunk[which * half : (which + 1) * half, s * sub_w : (s + 1) * sub_w] = own + ring_recv[
                which, ny - 1, s
            ].astype(F32)
    x_send[...] = chunk[...].astype(BF)

    def x_copy(i):
        other = (xh + i) % nx
        return pltpu.make_async_remote_copy(
            src_ref=x_send.at[pl.ds(pl.multiple_of(other * out_rows, out_rows), out_rows)],
            dst_ref=x_recv.at[i - 1],
            send_sem=x_ssem.at[i - 1], recv_sem=x_rsem.at[i - 1],
            device_id=(y * nx + other, me), device_id_type=MESH,
        )

    for i in range(1, nx):
        x_copy(i).start()

    wait_all(router_recv, 8, router_rsem)
    token_out[...] = dot(place8[...], router_recv[...], precision=lax.Precision.HIGHEST)[:, :1]

    wait_all(gate_send, 8, gate_ssem)
    wait_all(router_send, 8, router_ssem)

    @pl.loop(0, steps)
    def _(d):
        wait_all(send.at[d], msg, send_sem.at[d])

    @pl.loop(0, ny - 1)
    def _(k):
        for which in range(2):
            for s in range(SUBS):
                ring_copy(which, k, s).wait_send()

    grad = chunk[pl.ds(pl.multiple_of(xh * out_rows, out_rows), out_rows), :]
    for i in range(1, nx):
        x_copy(i).wait_recv()
        grad = grad + x_recv[i - 1].astype(F32)
    grad_out[...] = grad
    for i in range(1, nx):
        x_copy(i).wait_send()


def shards(nx, cotangent, routes, gate_weight, down_weight, saved_pre):
    peers = lax.axis_size("exp")
    ny = lax.axis_size("rep") // nx
    tokens, model = cotangent.shape
    slots, double = saved_pre.shape[2:]
    width = double // 2
    half = model // ny // 2
    steps = ny // 2
    out_rows = model // (ny * nx)
    msg = GROUP * CAP
    block = GROUP * msg
    vmem = pl.BlockSpec(memory_space=pltpu.VMEM)
    dma = pltpu.SemaphoreType.DMA
    grad, pairs, token = pl.pallas_call(
        functools.partial(kernel, ny, nx, peers),
        out_shape=(
            jax.ShapeDtypeStruct((out_rows, width), F32),
            jax.ShapeDtypeStruct((slots, double), BF),
            jax.ShapeDtypeStruct((tokens, 1), F32),
        ),
        in_specs=[vmem, vmem, vmem, pl.BlockSpec(memory_space=pl.ANY), vmem],
        out_specs=(vmem, vmem, vmem),
        scratch_shapes=[
            pltpu.VMEM((model, width), BF),
            pltpu.VMEM((steps, peers * msg, half // 2), BF),
            pltpu.VMEM((steps, peers * msg, half // 2), BF),
            pltpu.VMEM((steps, slots, 4 * half), BF),
            pltpu.VMEM((tokens, slots), BF),
            pltpu.VMEM((tokens, peers * 8), F32),
            pltpu.VMEM((block, block), BF),
            pltpu.VMEM((slots, peers * 8), F32),
            pltpu.VMEM((peers * 8, 128), F32),
            pltpu.VMEM((peers * 8, 128), F32),
            pltpu.VMEM((peers * 8, 128), F32),
            pltpu.VMEM((peers * 8, 128), F32),
            pltpu.VMEM((slots, width), F32),
            pltpu.VMEM((slots, 1), F32),
            pltpu.VMEM((slots, width), BF),
            pltpu.VMEM((slots, width), F32),
            pltpu.VMEM((2, ny - 1, SUBS, half, width // SUBS), BF),
            pltpu.VMEM((2, ny, SUBS, half, width // SUBS), BF),
            pltpu.VMEM((2 * half, width), F32),
            pltpu.VMEM((2 * half, width), BF),
            pltpu.VMEM((nx - 1, out_rows, width), BF),
            dma, dma((steps,)), dma((steps,)), dma, dma, dma, dma,
            dma((2, ny - 1, SUBS)), dma((2, ny - 1, SUBS)), dma((nx - 1,)), dma((nx - 1,)),
        ],
        compiler_params=pltpu.CompilerParams(
            collective_id=0, has_side_effects=True, vmem_limit_bytes=56 * 1024 * 1024
        ),
        cost_estimate=pl.CostEstimate(
            flops=4 * slots * model * width, bytes_accessed=12 * 1024 * 1024, transcendentals=0
        ),
        name="expert_backward",
    )(cotangent, routes, gate_weight, down_weight[0], saved_pre[0, 0])
    return grad[None], pairs[None, None], token


def solution(mesh):
    nx = 4 if mesh.shape["rep"] == 32 else 2
    in_specs = (
        P(("rep", "exp"), None),
        P(("rep", "exp"), None),
        P(("rep", "exp"), None),
        P("exp", None, None),
        P("rep", "exp", None, None),
    )
    out_specs = (P("exp", "rep", None), P("rep", "exp", None, None), P(("rep", "exp"), None))
    return jax.shard_map(
        functools.partial(shards, nx), mesh=mesh, in_specs=in_specs, out_specs=out_specs,
        check_vma=False,
    )
```

time: 369 us -> 147 us (0.40)
  waiting for transfers between devices: 282 us -> 0 us
  Pallas kernels: 0 us -> 138 us
  blocking collectives: 26.1 us -> 0 us
  starting transfers between devices: 19.3 us -> 0 us
  between operations: 14.1 us -> 0.64 us
  matrix products: 11.6 us -> 0 us
  other arithmetic: 8.96 us -> 0 us
  local copies, waits for them, and re-layouts: 3.98 us -> 7.88 us
    reduce_scatter x1 -> x0, waiting for transfers between devices: 232 us -> none  [shards(): lax.psum_scatter(partial_value.astype(jnp.bfloat16), 'rep', scatter_dimen...]
    pallas_call x0 -> x1, Pallas kernels: none -> 138 us  [shards(): pl.pallas_call(functools.partial(kernel, ny, nx, peers), out_shape=(jax.S...]
    all_to_all x1 -> x0, waiting for transfers between devices: 49.6 us -> none  [shards(): lax.all_to_all(outgoing.reshape(peers, capacity, -1), 'exp', split_axis=0...]
    all_to_all x2 -> x0, blocking collectives: 26.1 us -> none  [the longest x1 14.8 us: shards(): lax.all_to_all(router.reshape(peers, capacity), 'exp', split_axis=0, conc...]
    all_to_all x1 -> x0, starting transfers between devices: 19.3 us -> none  [shards(): lax.all_to_all(outgoing.reshape(peers, capacity, -1), 'exp', split_axis=0...]
    dot_general x3 -> x0, matrix products: 11.6 us -> none  [the longest x1 6 us: shards(): lax.dot_general(received, scaled, (((0,), (0,)), ((), ())), preferred_ele...]
    unnamed x6 -> x5, local copies, waits for them, and re-layouts: 0.02 us -> 7.88 us
  transfers between devices with their start and end apart: 2 -> 0, of which waited for: 2 -> 0; matrix products, arithmetic and copies ran while one was open for 1% -> 0% of each run, Pallas kernels for 0% -> 0%
where the time goes in v1:
time: 147 us; the launch traced here: 146 us
  Pallas kernels  138 us (94%)
  local copies, waits for them, and re-layouts  7.88 us (5%)
    pallas_call x1, Pallas kernels, shards(): pl.pallas_call(functools.partial(kernel, ny, nx, peers), out_shape=(jax.S...  138 us
    unnamed x5, local copies, waits for them, and re-layouts  7.88 us

profile of v1, /device:TPU:1, one launch (start us, length us, event | category | flops | bytes accessed | tf_op | source)
XLA Modules:
  0.0 146.4 jit_solution(357734429103285757)
XLA Ops:
  0.6 1.4 copy.8.routes
  2.0 1.4 copy.9.gate
  3.4 137.9 %expert_backward.1 = (f32[128,768]{1,0:T(8,128)}, bf16[192,1536]{1,0:T(8,128)(2,1)}, f32[128,1]{1,0:T(8,128)}) custom-call(bf16[128,4096]{1,0:T(8,128)(2,1)} %cot.1, s32[128,1]{1,0:T(8,128)} %copy.8.routes, f32[128,1]{1,0:T(8,128)} %copy.9.gate, bf16[4096,768]{1,0:T(8,128)(2,1)} %bitcast.6, bf16[192,1536]{1,0:T(8,128)(2,1)} %bitcast.7), custom_call_target="tpu_custom_call" | custom-call | flops 2415919104 | bytes 12582912 | tf_op jit(solution)/shard_map/expert_backward/pallas_call | solution.py:308
  141.3 1.4 copy.10
  142.8 1.8 %copy.13 = f32[1,128,768]{2,1,0:T(8,128)} copy(f32[1,128,768]{2,1,0:T(8,128)} %bitcast.5) | data formatting | bytes 786432
  144.5 1.9 %copy.14 = bf16[1,1,192,1536]{3,2,1,0:T(8,128)(2,1)} copy(bf16[1,1,192,1536]{3,2,1,0:T(8,128)(2,1)} %bitcast.4) | data formatting | bytes 1179648

commit v2 on v1

v2 whole, which is shorter than its diff:
```python
import functools

import jax
import jax.numpy as jnp
from jax import lax
from jax.experimental import pallas as pl
from jax.experimental.pallas import tpu as pltpu
from jax.sharding import PartitionSpec as P

MESH = pl.DeviceIdType.MESH
BF = jnp.bfloat16
F32 = jnp.float32
CAP = 6
GROUP = 8
WIDTHS = (384, 256, 128)


def dot(a, b, lhs=1, **kw):
    return lax.dot_general(a, b, (((lhs,), (0,)), ((), ())), preferred_element_type=F32, **kw)


def iota(shape, dim):
    return lax.broadcasted_iota(jnp.int32, shape, dim).astype(F32)


def kernel(
    ny, nx, peers, widths,
    cot, routes, gate, weight_hbm, saved,
    grad_out, pair_out, token_out,
    weight, send, recv, edge_send, edge_recv, arrived, place6, place8, swap, edge, pick, select,
    router_send, router_recv, hidden, scale, scaled, pulled,
    ring_send0, ring_recv0, ring_send1, ring_recv1, chunk, x_send0, x_recv0, x_send1, x_recv1,
    cross_send, cross_recv, column_send, column_recv,
    weight_sem, send_sem, recv_sem, edge_ssem, edge_rsem, router_ssem, router_rsem,
    ring_ssem, ring_rsem, x_ssem, x_rsem, cross_ssem, cross_rsem, column_ssem, column_rsem,
):
    tokens = cot.shape[0]
    slots = peers * CAP
    groups = peers // GROUP
    width = weight.shape[1]
    span = cot.shape[1] // ny
    half = span // 2
    rows = GROUP * CAP
    block = GROUP * rows
    msg = GROUP * CAP
    lanes = 128
    piece = half // nx
    ring_send, ring_recv = (ring_send0, ring_send1), (ring_recv0, ring_recv1)
    x_send, x_recv = (x_send0, x_send1), (x_recv0, x_recv1)
    starts = (0, widths[0], widths[0] + widths[1])
    cross_at = starts[2]
    last = ny - 1
    rep, me = lax.axis_index("rep"), lax.axis_index("exp")
    y, xh = rep // nx, rep % nx
    right = ((y + 1) % ny) * nx + xh
    left = ((y + ny - 1) % ny) * nx + xh

    weight_copy = pltpu.make_async_copy(weight_hbm, weight, weight_sem)
    weight_copy.start()

    barrier = pltpu.get_barrier_semaphore()

    @pl.loop(1, peers)
    def _(i):
        pl.semaphore_signal(
            barrier, inc=1, device_id=(rep, (me + i) % peers), device_id_type=MESH
        )

    for other in (left, right):
        pl.semaphore_signal(barrier, inc=1, device_id=(other, me), device_id_type=MESH)
    for i in range(1, nx):
        pl.semaphore_signal(
            barrier, inc=1, device_id=(y * nx + (xh + i) % nx, me), device_id_type=MESH
        )

    def chunk_at(which, k):
        return (y + ny - 1 - k) % ny if which == 0 else (y + 1 + k) % ny

    eye = iota((tokens, tokens), 0) == iota((tokens, tokens), 1)

    def as_column(row):
        return jnp.sum(jnp.where(eye, row, 0.0), axis=1, keepdims=True)

    ids = as_column(routes[...].astype(F32))
    one_hot = ids == iota((tokens, peers), 1)
    below = (iota((tokens, tokens), 0) > iota((tokens, tokens), 1)).astype(F32).astype(BF)
    earlier = dot(below, one_hot.astype(F32).astype(BF))
    position = jnp.sum(jnp.where(one_hot, earlier, 0.0), axis=1, keepdims=True)
    place6[...] = (ids * CAP + position == iota((tokens, slots), 1)).astype(F32).astype(BF)
    place8[...] = (ids * 8 + position == iota((tokens, peers * 8), 1)).astype(F32)
    gates = jnp.broadcast_to(as_column(gate[...]), (tokens, lanes)).astype(BF)

    r = iota((block, 1), 0)
    a = jnp.floor((r + 0.5) * (1.0 / rows))
    ab = jnp.floor((r + 0.5) * (1.0 / CAP))
    source = (ab - GROUP * a) * rows + a * CAP + (r - CAP * ab)
    swap[...] = (source == iota((block, block), 1)).astype(F32).astype(BF)
    r = iota((GROUP * 32, 1), 0)
    a = jnp.floor((r + 0.5) * (1.0 / 32))
    m = r - 32 * a
    b = jnp.floor((m + 0.5) * (1.0 / CAP))
    source = b * rows + a * CAP + (m - CAP * b)
    edge[...] = (source == iota((GROUP * 32, 5 * rows), 1)).astype(F32).astype(BF)
    for which in range(2):
        r = iota((half, half), 1)
        owner = jnp.floor((r + 0.5) * (1.0 / piece))
        source = r + piece * (owner + which)
        for q in range(2):
            pick[which, q * half : (q + 1) * half, :] = (
                (iota((half, half), 0) + q * half == source).astype(F32).astype(BF)
            )
    r = iota((slots, 1), 0)
    spread = r + (8 - CAP) * jnp.floor((r + 0.5) * (1.0 / CAP))
    select[...] = (spread == iota((slots, peers * 8), 1)).astype(F32)

    def half_columns(which, k):
        at = pl.multiple_of(chunk_at(which, k) * span, span)
        return dot(cot[:, pl.ds(at, span)], pick[which]).astype(BF)

    def arrange(matrix, parts):
        placed = dot(place6[...], jnp.concatenate(parts, axis=1), 0).astype(BF)
        count = placed.shape[1] // lanes
        stacked = [
            [placed[g * rows : (g + 1) * rows, c * lanes : (c + 1) * lanes] for c in range(count)]
            for g in range(groups)
        ]
        stacked = jnp.concatenate([jnp.concatenate(s, axis=0) for s in stacked], axis=1)
        return dot(matrix, stacked).astype(BF)

    def build(d):
        out = arrange(
            swap[...], [half_columns(w, 2 * d + 1 + i) for i in range(2) for w in range(2)]
        )
        for g in range(groups):
            send[d, g * block : (g + 1) * block, :] = out[:, g * lanes : (g + 1) * lanes]

    def build_edge(e, k):
        out = arrange(edge[...], [half_columns(w, k) for w in range(2)] + [gates])
        size = GROUP * 32
        for g in range(groups):
            edge_send[e, g * size : (g + 1) * size, :] = out[:, g * lanes : (g + 1) * lanes]

    def router_copy(peer):
        return pltpu.make_async_remote_copy(
            src_ref=router_send.at[pl.ds(pl.multiple_of(peer * 8, 8), 8)],
            dst_ref=router_recv.at[pl.ds(pl.multiple_of(me * 8, 8), 8)],
            send_sem=router_ssem, recv_sem=router_rsem,
            device_id=(rep, peer), device_id_type=MESH,
        )

    def row_copy(d, peer):
        return pltpu.make_async_remote_copy(
            src_ref=send.at[d, pl.ds(pl.multiple_of(peer * msg, msg), msg)],
            dst_ref=recv.at[d, pl.ds(pl.multiple_of(me * msg, msg), msg)],
            send_sem=send_sem.at[d], recv_sem=recv_sem.at[d],
            device_id=(rep, peer), device_id_type=MESH,
        )

    def edge_copy(e, peer):
        return pltpu.make_async_remote_copy(
            src_ref=edge_send.at[e, pl.ds(pl.multiple_of(peer * 32, 32), 32)],
            dst_ref=edge_recv.at[e, pl.ds(pl.multiple_of(me * 32, 32), 32)],
            send_sem=edge_ssem.at[e], recv_sem=edge_rsem.at[e],
            device_id=(rep, peer), device_id_type=MESH,
        )

    def to_peers(copy):
        @pl.loop(1, peers)
        def _(i):
            copy((me + i) % peers).start()

    def wait_all(buffer, size, sem):
        part = buffer.at[pl.ds(0, (peers - 1) * size)]
        pltpu.make_async_copy(part, part, sem).wait()

    build_edge(0, 0)
    pl.semaphore_wait(barrier, peers - 1 + 2 + nx - 1)
    to_peers(lambda peer: edge_copy(0, peer))
    mine = pl.ds(pl.multiple_of(me * msg, msg), msg)
    mine32 = pl.ds(pl.multiple_of(me * 32, 32), 32)
    mine8 = pl.ds(pl.multiple_of(me * 8, 8), 8)
    edge_recv[0, mine32, :] = edge_send[0, mine32, :]

    @pl.loop(0, last // 2)
    def _(d):
        build(d)
        recv[d, mine, :] = send[d, mine, :]

    build_edge(1, last)
    edge_recv[1, mine32, :] = edge_send[1, mine32, :]

    g = saved[:, :width].astype(F32)
    u = saved[:, width:].astype(F32)
    hidden[...] = g * jax.nn.sigmoid(g) * u
    pulled[...] = jnp.zeros_like(pulled)
    weight_copy.wait()

    def take_edge(e, k):
        wait_all(edge_recv.at[e], 32, edge_rsem.at[e])
        size = GROUP * 32
        stacked = jnp.concatenate(
            [edge_recv[e, g * size : (g + 1) * size, :] for g in range(groups)], axis=1
        )
        out = dot(edge[...], stacked, 0)
        for g in range(groups):
            for c in range(4):
                arrived[k, g * rows : (g + 1) * rows, c * lanes : (c + 1) * lanes] = out[
                    c * rows : (c + 1) * rows, g * lanes : (g + 1) * lanes
                ].astype(BF)
        return out

    def take(d):
        wait_all(recv.at[d], msg, recv_sem.at[d])
        stacked = jnp.concatenate(
            [recv[d, g * block : (g + 1) * block, :] for g in range(groups)], axis=1
        )
        out = dot(swap[...], stacked).astype(BF)
        for g in range(groups):
            for c in range(GROUP):
                at = c % 4 * lanes
                arrived[2 * d + 1 + c // 4, g * rows : (g + 1) * rows, at : at + lanes] = out[
                    c * rows : (c + 1) * rows, g * lanes : (g + 1) * lanes
                ]

    def ring_copy(which, k, s):
        return pltpu.make_async_remote_copy(
            src_ref=ring_send[s].at[which, k], dst_ref=ring_recv[s].at[which, k],
            send_sem=ring_ssem.at[which, k, s], recv_sem=ring_rsem.at[which, k, s],
            device_id=((left if which else right), me), device_id_type=MESH,
        )

    def column_copy(which, k):
        return pltpu.make_async_remote_copy(
            src_ref=column_send.at[which, k], dst_ref=column_recv.at[which, k],
            send_sem=column_ssem.at[which, k], recv_sem=column_rsem.at[which, k],
            device_id=((left if which else right), me), device_id_type=MESH,
        )

    def cross_copy(which, k, i):
        other = (xh + i) % nx
        return pltpu.make_async_remote_copy(
            src_ref=cross_send.at[which, k, pl.ds(pl.multiple_of(other * piece, piece), piece)],
            dst_ref=cross_recv.at[which, k, i - 1],
            send_sem=cross_ssem.at[which, k, i - 1], recv_sem=cross_rsem.at[which, k, i - 1],
            device_id=(y * nx + other, me), device_id_type=MESH,
        )

    def x_copy(which, s, i):
        other = (xh + i) % nx
        return pltpu.make_async_remote_copy(
            src_ref=x_send[s].at[which, pl.ds(pl.multiple_of(other * piece, piece), piece)],
            dst_ref=x_recv[s].at[which, i - 1],
            send_sem=x_ssem.at[which, s, i - 1], recv_sem=x_rsem.at[which, s, i - 1],
            device_id=(y * nx + other, me), device_id_type=MESH,
        )

    def term(k, which, at, size):
        part = arrived[k, :, which * half : (which + 1) * half]
        return dot(part, scaled[:, at : at + size], 0)

    def ring_sum(k, which, s, first=False):
        own = term(k, which, starts[s], widths[s])
        if not first:
            ring_copy(which, k - 1, s).wait_recv()
            own = own + ring_recv[s][which, k - 1].astype(F32)
        return own

    def ring_step(k, first=False):
        for s in range(2):
            for which in range(2):
                ring_send[s][which, k] = ring_sum(k, which, s, first).astype(BF)
                ring_copy(which, k, s).start()

    def cross_step(k):
        for which in range(2):
            cross_send[which, k] = term(k, which, cross_at, widths[2]).astype(BF)
            for i in range(1, nx):
                cross_copy(which, k, i).start()

    own_piece = pl.ds(pl.multiple_of(xh * piece, piece), piece)

    def column_step(k, first=False, final=False):
        for which in range(2):
            total = cross_send[which, k, own_piece, :].astype(F32)
            for i in range(1, nx):
                cross_copy(which, k, i).wait_recv()
                total = total + cross_recv[which, k, i - 1].astype(F32)
            if not first:
                column_copy(which, k - 1).wait_recv()
                total = total + column_recv[which, k - 1].astype(F32)
            if final:
                grad_out[which * piece : (which + 1) * piece, cross_at:] = total
            else:
                column_send[which, k] = total.astype(BF)
                column_copy(which, k).start()

    def pull(k):
        total = pulled[...]
        for w in range(2):
            at = chunk_at(w, k) * span + w * piece
            part = jnp.concatenate(
                [
                    weight[pl.ds(pl.multiple_of(at + 2 * piece * q, piece), piece), :]
                    for q in range(nx)
                ],
                axis=0,
            )
            total = total + dot(arrived[k, :, w * half : (w + 1) * half], part)
        pulled[...] = total

    out = take_edge(0, 0)
    for g in range(groups):
        scale[g * rows : (g + 1) * rows, :] = out[4 * rows :, g * lanes : (g + 1) * lanes]
    scaled[...] = (scale[:, :1] * hidden[...]).astype(BF)
    ring_step(0, first=True)
    cross_step(0)
    to_peers(lambda peer: row_copy(0, peer))
    pull(0)

    def pair_of_steps(d, first):
        take(d)
        k = 2 * d + 1
        ring_step(k)
        cross_step(k)
        column_step(k - 1, first)

        if first:
            to_peers(lambda peer: row_copy(1, peer))
        else:

            @pl.when(d < last // 2 - 1)
            def _():
                to_peers(lambda peer: row_copy(d + 1, peer))

            @pl.when(d == last // 2 - 1)
            def _():
                to_peers(lambda peer: edge_copy(1, peer))

        cross_step(k + 1)
        pull(k)
        pull(k + 1)
        ring_step(k + 1)
        column_step(k)

    pair_of_steps(0, True)

    @pl.loop(1, last // 2)
    def _(d):
        pair_of_steps(d, False)

    take_edge(1, last)
    cross_step(last)
    pull(last)

    router = jnp.sum(pulled[...] * hidden[...], axis=1, keepdims=True)
    router_send[...] = dot(
        select[...], jnp.broadcast_to(router, (slots, lanes)), 0, precision=lax.Precision.HIGHEST
    )
    to_peers(router_copy)
    router_recv[mine8, :] = router_send[mine8, :]
    column_step(last - 1)
    g = saved[:, :width].astype(F32)
    u = saved[:, width:].astype(F32)
    sg = jax.nn.sigmoid(g)
    dh = scale[:, :1] * pulled[...]
    pair_out[:, :width] = (dh * u * sg * (1.0 + g * (1.0 - sg))).astype(BF)
    pair_out[:, width:] = (dh * g * sg).astype(BF)

    for s in range(2):
        for which in range(2):
            own = ring_sum(last, which, s)
            chunk[which, :, starts[s] : starts[s + 1]] = own
            x_send[s][which] = own.astype(BF)
            for i in range(1, nx):
                x_copy(which, s, i).start()

    column_step(last, final=True)
    wait_all(router_recv, 8, router_rsem)
    token = dot(place8[...], router_recv[...], precision=lax.Precision.HIGHEST)
    token_out[...] = jnp.sum(jnp.where(eye, token, 0.0), axis=0, keepdims=True)

    wait_all(router_send, 8, router_ssem)
    for e in range(2):
        wait_all(edge_send.at[e], 32, edge_ssem.at[e])

    @pl.loop(0, last // 2)
    def _(d):
        wait_all(send.at[d], msg, send_sem.at[d])

    @pl.loop(0, last)
    def _(k):
        for which in range(2):
            column_copy(which, k).wait_send()
            for s in range(2):
                ring_copy(which, k, s).wait_send()

    @pl.loop(0, ny)
    def _(k):
        for which in range(2):
            for i in range(1, nx):
                cross_copy(which, k, i).wait_send()

    for s in range(2):
        for which in range(2):
            total = chunk[which, own_piece, starts[s] : starts[s + 1]]
            for i in range(1, nx):
                x_copy(which, s, i).wait_recv()
                total = total + x_recv[s][which, i - 1].astype(F32)
            grad_out[which * piece : (which + 1) * piece, starts[s] : starts[s + 1]] = total
            for i in range(1, nx):
                x_copy(which, s, i).wait_send()


def shards(nx, widths, cotangent, routes, gate_weight, down_weight, saved_pre):
    peers = lax.axis_size("exp")
    ny = lax.axis_size("rep") // nx
    tokens, model = cotangent.shape
    slots, double = saved_pre.shape[2:]
    width = double // 2
    half = model // ny // 2
    last = ny - 1
    pairs = last // 2
    piece = half // nx
    msg = GROUP * CAP
    block = GROUP * msg
    vmem = pl.BlockSpec(memory_space=pltpu.VMEM)
    dma = pltpu.SemaphoreType.DMA
    wa, wb, wc = widths
    grad, pair, token = pl.pallas_call(
        functools.partial(kernel, ny, nx, peers, widths),
        out_shape=(
            jax.ShapeDtypeStruct((2 * piece, width), F32),
            jax.ShapeDtypeStruct((slots, double), BF),
            jax.ShapeDtypeStruct((1, tokens), F32),
        ),
        in_specs=[vmem, vmem, vmem, pl.BlockSpec(memory_space=pl.ANY), vmem],
        out_specs=(vmem, vmem, vmem),
        scratch_shapes=[
            pltpu.VMEM((model, width), BF),
            pltpu.VMEM((pairs, peers * msg, 128), BF),
            pltpu.VMEM((pairs, peers * msg, 128), BF),
            pltpu.VMEM((2, peers * 32, 128), BF),
            pltpu.VMEM((2, peers * 32, 128), BF),
            pltpu.VMEM((ny, slots, 2 * half), BF),
            pltpu.VMEM((tokens, slots), BF),
            pltpu.VMEM((tokens, peers * 8), F32),
            pltpu.VMEM((block, block), BF),
            pltpu.VMEM((GROUP * 32, 5 * msg), BF),
            pltpu.VMEM((2, 2 * half, half), BF),
            pltpu.VMEM((slots, peers * 8), F32),
            pltpu.VMEM((peers * 8, 128), F32),
            pltpu.VMEM((peers * 8, 128), F32),
            pltpu.VMEM((slots, width), F32),
            pltpu.VMEM((slots, 128), F32),
            pltpu.VMEM((slots, width), BF),
            pltpu.VMEM((slots, width), F32),
            pltpu.VMEM((2, last, half, wa), BF),
            pltpu.VMEM((2, last, half, wa), BF),
            pltpu.VMEM((2, last, half, wb), BF),
            pltpu.VMEM((2, last, half, wb), BF),
            pltpu.VMEM((2, half, wa + wb), F32),
            pltpu.VMEM((2, half, wa), BF),
            pltpu.VMEM((2, nx - 1, piece, wa), BF),
            pltpu.VMEM((2, half, wb), BF),
            pltpu.VMEM((2, nx - 1, piece, wb), BF),
            pltpu.VMEM((2, ny, half, wc), BF),
            pltpu.VMEM((2, ny, nx - 1, piece, wc), BF),
            pltpu.VMEM((2, last, piece, wc), BF),
            pltpu.VMEM((2, last, piece, wc), BF),
            dma, dma((pairs,)), dma((pairs,)), dma((2,)), dma((2,)), dma, dma,
            dma((2, last, 2)), dma((2, last, 2)), dma((2, 2, nx - 1)), dma((2, 2, nx - 1)),
            dma((2, ny, nx - 1)), dma((2, ny, nx - 1)), dma((2, last)), dma((2, last)),
        ],
        compiler_params=pltpu.CompilerParams(
            collective_id=0, has_side_effects=True, vmem_limit_bytes=56 * 1024 * 1024
        ),
        cost_estimate=pl.CostEstimate(
            flops=4 * slots * model * width, bytes_accessed=12 * 1024 * 1024, transcendentals=0
        ),
        name="expert_backward",
    )(
        cotangent,
        routes.reshape(1, tokens),
        gate_weight.reshape(1, tokens),
        down_weight[0],
        saved_pre[0, 0],
    )
    return grad[None], pair[None, None], token.reshape(tokens, 1)


def solution(mesh):
    nx = 4 if mesh.shape["rep"] == 32 else 2
    in_specs = (
        P(("rep", "exp"), None),
        P(("rep", "exp"), None),
        P(("rep", "exp"), None),
        P("exp", None, None),
        P("rep", "exp", None, None),
    )
    out_specs = (P("exp", "rep", None), P("rep", "exp", None, None), P(("rep", "exp"), None))
    return jax.shard_map(
        functools.partial(shards, nx, WIDTHS), mesh=mesh, in_specs=in_specs, out_specs=out_specs,
        check_vma=False,
    )
```

time: 147 us -> 120 us (0.82)
  Pallas kernels: 138 us -> 114 us
  local copies, waits for them, and re-layouts: 7.88 us -> 4.77 us
    pallas_call x1, Pallas kernels: 138 us -> 114 us  [shards(): pl.pallas_call(functools.partial(kernel, ny, nx, peers, widths), out_shap...]
    unnamed x5 -> x3, local copies, waits for them, and re-layouts: 7.88 us -> 4.77 us
where the time goes in v2:
time: 120 us; the launch traced here: 119 us
  Pallas kernels  114 us (95%)
  local copies, waits for them, and re-layouts  4.77 us (4%)
    pallas_call x1, Pallas kernels, shards(): pl.pallas_call(functools.partial(kernel, ny, nx, peers, widths), out_shap...  114 us
    unnamed x3, local copies, waits for them, and re-layouts  4.77 us

profile of v2, /device:TPU:1, one launch (start us, length us, event | category | flops | bytes accessed | tf_op | source)
XLA Modules:
  0.0 119.3 jit_solution(17175292061381121693)
XLA Ops:
  0.6 113.9 %expert_backward.1 = (f32[128,768]{1,0:T(8,128)}, bf16[192,1536]{1,0:T(8,128)(2,1)}, f32[1,128]{1,0:T(1,128)}) custom-call(bf16[128,4096]{1,0:T(8,128)(2,1)} %cot.1, s32[1,128]{1,0:T(1,128)} %bitcast.11, f32[1,128]{1,0:T(1,128)} %bitcast.12, bf16[4096,768]{1,0:T(8,128)(2,1)} %bitcast.9, bf16[192,1536]{1,0:T(8,128)(2,1)} %bitcast.10), custom_call_target="tpu_custom_call" | custom-call | flops 2415919104 | bytes 12582912 | tf_op jit(solution)/shard_map/expert_backward/pallas_call | solution.py:429
  114.6 1.8 %copy.11 = f32[1,128,768]{2,1,0:T(8,128)} copy(f32[1,128,768]{2,1,0:T(8,128)} %bitcast.8) | data formatting | bytes 786432
  116.3 1.9 %copy.12 = bf16[1,1,192,1536]{3,2,1,0:T(8,128)(2,1)} copy(bf16[1,1,192,1536]{3,2,1,0:T(8,128)(2,1)} %bitcast.7) | data formatting | bytes 1179648
  118.2 1.1 copy.13

commit v3 on v2

--- a/solution.py
+++ b/solution.py
@@ -12,7 +12,10 @@
 F32 = jnp.float32
 CAP = 6
 GROUP = 8
-WIDTHS = (384, 256, 128)
+SUB = 128
+CROSS = 128
+AHEAD = 3
+LAG = 2
 
 
 def dot(a, b, lhs=1, **kw):
@@ -24,12 +27,12 @@
 
 
 def kernel(
-    ny, nx, peers, widths,
+    ny, nx, peers,
     cot, routes, gate, weight_hbm, saved,
     grad_out, pair_out, token_out,
     weight, send, recv, edge_send, edge_recv, arrived, place6, place8, swap, edge, pick, select,
     router_send, router_recv, hidden, scale, scaled, pulled,
-    ring_send0, ring_recv0, ring_send1, ring_recv1, chunk, x_send0, x_recv0, x_send1, x_recv1,
+    own, ring_send, ring_recv, chunk, x_send, x_recv,
     cross_send, cross_recv, column_send, column_recv,
     weight_sem, send_sem, recv_sem, edge_ssem, edge_rsem, router_ssem, router_rsem,
     ring_ssem, ring_rsem, x_ssem, x_rsem, cross_ssem, cross_rsem, column_ssem, column_rsem,
@@ -45,10 +48,8 @@
     msg = GROUP * CAP
     lanes = 128
     piece = half // nx
-    ring_send, ring_recv = (ring_send0, ring_send1), (ring_recv0, ring_recv1)
-    x_send, x_recv = (x_send0, x_send1), (x_recv0, x_recv1)
-    starts = (0, widths[0], widths[0] + widths[1])
-    cross_at = starts[2]
+    cross_at = width - CROSS
+    subs = cross_at // SUB
     last = ny - 1
     rep, me = lax.axis_index("rep"), lax.axis_index("exp")
     y, xh = rep // nx, rep % nx
@@ -87,14 +88,8 @@
     earlier = dot(below, one_hot.astype(F32).astype(BF))
     position = jnp.sum(jnp.where(one_hot, earlier, 0.0), axis=1, keepdims=True)
     place6[...] = (ids * CAP + position == iota((tokens, slots), 1)).astype(F32).astype(BF)
-    place8[...] = (ids * 8 + position == iota((tokens, peers * 8), 1)).astype(F32)
     gates = jnp.broadcast_to(as_column(gate[...]), (tokens, lanes)).astype(BF)
 
-    r = iota((block, 1), 0)
-    a = jnp.floor((r + 0.5) * (1.0 / rows))
-    ab = jnp.floor((r + 0.5) * (1.0 / CAP))
-    source = (ab - GROUP * a) * rows + a * CAP + (r - CAP * ab)
-    swap[...] = (source == iota((block, block), 1)).astype(F32).astype(BF)
     r = iota((GROUP * 32, 1), 0)
     a = jnp.floor((r + 0.5) * (1.0 / 32))
     m = r - 32 * a
@@ -109,10 +104,6 @@
             pick[which, q * half : (q + 1) * half, :] = (
                 (iota((half, half), 0) + q * half == source).astype(F32).astype(BF)
             )
-    r = iota((slots, 1), 0)
-    spread = r + (8 - CAP) * jnp.floor((r + 0.5) * (1.0 / CAP))
-    select[...] = (spread == iota((slots, peers * 8), 1)).astype(F32)
-
     def half_columns(which, k):
         at = pl.multiple_of(chunk_at(which, k) * span, span)
         return dot(cot[:, pl.ds(at, span)], pick[which]).astype(BF)
@@ -167,7 +158,8 @@
     def to_peers(copy):
         @pl.loop(1, peers)
         def _(i):
-            copy((me + i) % peers).start()
+            off = (i % 2) * ((i + 1) // 2) + ((i + 1) % 2) * (peers - i // 2)
+            copy((me + off) % peers).start()
 
     def wait_all(buffer, size, sem):
         part = buffer.at[pl.ds(0, (peers - 1) * size)]
@@ -181,11 +173,22 @@
     mine8 = pl.ds(pl.multiple_of(me * 8, 8), 8)
     edge_recv[0, mine32, :] = edge_send[0, mine32, :]
 
+    r = iota((block, 1), 0)
+    a = jnp.floor((r + 0.5) * (1.0 / rows))
+    ab = jnp.floor((r + 0.5) * (1.0 / CAP))
+    source = (ab - GROUP * a) * rows + a * CAP + (r - CAP * ab)
+    swap[...] = (source == iota((block, block), 1)).astype(F32).astype(BF)
+    place8[...] = (ids * 8 + position == iota((tokens, peers * 8), 1)).astype(F32)
+    r = iota((slots, 1), 0)
+    spread = r + (8 - CAP) * jnp.floor((r + 0.5) * (1.0 / CAP))
+    select[...] = (spread == iota((slots, peers * 8), 1)).astype(F32)
+
     @pl.loop(0, last // 2)
     def _(d):
         build(d)
         recv[d, mine, :] = send[d, mine, :]
 
+    to_peers(lambda peer: row_copy(0, peer))
     build_edge(1, last)
     edge_recv[1, mine32, :] = edge_send[1, mine32, :]
 
@@ -224,14 +227,14 @@
 
     def ring_copy(which, k, s):
         return pltpu.make_async_remote_copy(
-            src_ref=ring_send[s].at[which, k], dst_ref=ring_recv[s].at[which, k],
+            src_ref=ring_send.at[which, k, s], dst_ref=ring_recv.at[which, k, s],
             send_sem=ring_ssem.at[which, k, s], recv_sem=ring_rsem.at[which, k, s],
             device_id=((left if which else right), me), device_id_type=MESH,
         )
 
     def column_copy(which, k):
         return pltpu.make_async_remote_copy(
-            src_ref=column_send.at[which, k], dst_ref=column_recv.at[which, k],
+            src_ref=column_send.at[which, k], dst_ref=column_recv.at[which, k + 1],
             send_sem=column_ssem.at[which, k], recv_sem=column_rsem.at[which, k],
             device_id=((left if which else right), me), device_id_type=MESH,
         )
@@ -248,110 +251,119 @@
     def x_copy(which, s, i):
         other = (xh + i) % nx
         return pltpu.make_async_remote_copy(
-            src_ref=x_send[s].at[which, pl.ds(pl.multiple_of(other * piece, piece), piece)],
-            dst_ref=x_recv[s].at[which, i - 1],
+            src_ref=x_send.at[which, s, pl.ds(pl.multiple_of(other * piece, piece), piece)],
+            dst_ref=x_recv.at[which, s, i - 1],
             send_sem=x_ssem.at[which, s, i - 1], recv_sem=x_rsem.at[which, s, i - 1],
             device_id=(y * nx + other, me), device_id_type=MESH,
         )
 
-    def term(k, which, at, size):
-        part = arrived[k, :, which * half : (which + 1) * half]
-        return dot(part, scaled[:, at : at + size], 0)
-
-    def ring_sum(k, which, s, first=False):
-        own = term(k, which, starts[s], widths[s])
-        if not first:
+    def summed(k, which, s):
+        total = own[which, k, :, s * SUB : (s + 1) * SUB]
+        if k > 0:
             ring_copy(which, k - 1, s).wait_recv()
-            own = own + ring_recv[s][which, k - 1].astype(F32)
-        return own
-
-    def ring_step(k, first=False):
-        for s in range(2):
-            for which in range(2):
-                ring_send[s][which, k] = ring_sum(k, which, s, first).astype(BF)
+            total = total + ring_recv[which, k - 1, s].astype(F32)
+        return total
+
+    def hop(k, s):
+        for which in range(2):
+            total = summed(k, which, s)
+            if k < last:
+                ring_send[which, k, s] = total.astype(BF)
                 ring_copy(which, k, s).start()
+            else:
+                chunk[which, s] = total
+                x_send[which, s] = total.astype(BF)
+                for i in range(1, nx):
+                    x_copy(which, s, i).start()
+
+    def hops(t, between=()):
+        todo = [(t, s) for s in range(AHEAD)] if t <= last else []
+        if t >= LAG:
+            todo += [(t - LAG, s) for s in range(AHEAD, subs)]
+        for n in range(max(len(todo), len(between))):
+            if n < len(todo):
+                hop(*todo[n])
+            if n < len(between):
+                between[n]()
+
+    def terms(k):
+        for which in range(2):
+            part = arrived[k, :, which * half : (which + 1) * half]
+            product = dot(part, scaled[...], 0)
+            own[which, k] = product[:, :cross_at]
+            cross_send[which, k] = product[:, cross_at:].astype(BF)
 
     def cross_step(k):
         for which in range(2):
-            cross_send[which, k] = term(k, which, cross_at, widths[2]).astype(BF)
             for i in range(1, nx):
                 cross_copy(which, k, i).start()
 
     own_piece = pl.ds(pl.multiple_of(xh * piece, piece), piece)
 
-    def column_step(k, first=False, final=False):
+    def column_step(k, final=False):
         for which in range(2):
             total = cross_send[which, k, own_piece, :].astype(F32)
             for i in range(1, nx):
                 cross_copy(which, k, i).wait_recv()
                 total = total + cross_recv[which, k, i - 1].astype(F32)
-            if not first:
+            if k > 0:
                 column_copy(which, k - 1).wait_recv()
-                total = total + column_recv[which, k - 1].astype(F32)
+                total = total + column_recv[which, k].astype(F32)
             if final:
                 grad_out[which * piece : (which + 1) * piece, cross_at:] = total
             else:
                 column_send[which, k] = total.astype(BF)
                 column_copy(which, k).start()
 
-    def pull(k):
-        total = pulled[...]
-        for w in range(2):
-            at = chunk_at(w, k) * span + w * piece
-            part = jnp.concatenate(
-                [
-                    weight[pl.ds(pl.multiple_of(at + 2 * piece * q, piece), piece), :]
-                    for q in range(nx)
-                ],
-                axis=0,
-            )
-            total = total + dot(arrived[k, :, w * half : (w + 1) * half], part)
-        pulled[...] = total
+    def pull(k, w):
+        at = chunk_at(w, k) * span + w * piece
+        part = jnp.concatenate(
+            [
+                weight[pl.ds(pl.multiple_of(at + 2 * piece * q, piece), piece), :]
+                for q in range(nx)
+            ],
+            axis=0,
+        )
+        pulled[...] += dot(arrived[k, :, w * half : (w + 1) * half], part)
 
     out = take_edge(0, 0)
+    to_peers(lambda peer: row_copy(1, peer))
     for g in range(groups):
         scale[g * rows : (g + 1) * rows, :] = out[4 * rows :, g * lanes : (g + 1) * lanes]
     scaled[...] = (scale[:, :1] * hidden[...]).astype(BF)
-    ring_step(0, first=True)
+    terms(0)
+    hops(0)
     cross_step(0)
-    to_peers(lambda peer: row_copy(0, peer))
-    pull(0)
-
-    def pair_of_steps(d, first):
+    pull(0, 0)
+    pull(0, 1)
+    for d in range(last // 2):
         take(d)
-        k = 2 * d + 1
-        ring_step(k)
-        cross_step(k)
-        column_step(k - 1, first)
-
-        if first:
-            to_peers(lambda peer: row_copy(1, peer))
-        else:
-
-            @pl.when(d < last // 2 - 1)
-            def _():
-                to_peers(lambda peer: row_copy(d + 1, peer))
-
-            @pl.when(d == last // 2 - 1)
-            def _():
-                to_peers(lambda peer: edge_copy(1, peer))
-
-        cross_step(k + 1)
-        pull(k)
-        pull(k + 1)
-        ring_step(k + 1)
-        column_step(k)
-
-    pair_of_steps(0, True)
-
-    @pl.loop(1, last // 2)
-    def _(d):
-        pair_of_steps(d, False)
+        if d < last // 2 - 2:
+            to_peers(functools.partial(row_copy, d + 2))
+        elif d == last // 2 - 2:
+            to_peers(functools.partial(edge_copy, 1))
+        for k in (2 * d + 1, 2 * d + 2):
+            terms(k)
+            hops(
+                k,
+                (
+                    functools.partial(cross_step, k),
+                    functools.partial(pull, k, 0),
+                    functools.partial(column_step, k - 1),
+                    functools.partial(pull, k, 1),
+                ),
+            )
 
     take_edge(1, last)
-    cross_step(last)
-    pull(last)
-
+    terms(last)
+    hops(
+        last,
+        (
+            functools.partial(cross_step, last),
+            functools.partial(pull, last, 0),
+            functools.partial(pull, last, 1),
+        ),
+    )
     router = jnp.sum(pulled[...] * hidden[...], axis=1, keepdims=True)
     router_send[...] = dot(
         select[...], jnp.broadcast_to(router, (slots, lanes)), 0, precision=lax.Precision.HIGHEST
@@ -359,6 +371,7 @@
     to_peers(router_copy)
     router_recv[mine8, :] = router_send[mine8, :]
     column_step(last - 1)
+    hops(last + 1)
     g = saved[:, :width].astype(F32)
     u = saved[:, width:].astype(F32)
     sg = jax.nn.sigmoid(g)
@@ -366,19 +379,15 @@
     pair_out[:, :width] = (dh * u * sg * (1.0 + g * (1.0 - sg))).astype(BF)
     pair_out[:, width:] = (dh * g * sg).astype(BF)
 
-    for s in range(2):
-        for which in range(2):
-            own = ring_sum(last, which, s)
-            chunk[which, :, starts[s] : starts[s + 1]] = own
-            x_send[s][which] = own.astype(BF)
-            for i in range(1, nx):
-                x_copy(which, s, i).start()
-
+    hops(last + 2)
     column_step(last, final=True)
     wait_all(router_recv, 8, router_rsem)
     token = dot(place8[...], router_recv[...], precision=lax.Precision.HIGHEST)
     token_out[...] = jnp.sum(jnp.where(eye, token, 0.0), axis=0, keepdims=True)
 
+    for t in range(last + 3, last + LAG + 1):
+        hops(t)
+
     wait_all(router_send, 8, router_ssem)
     for e in range(2):
         wait_all(edge_send.at[e], 32, edge_ssem.at[e])
@@ -391,7 +400,7 @@
     def _(k):
         for which in range(2):
             column_copy(which, k).wait_send()
-            for s in range(2):
+            for s in range(subs):
                 ring_copy(which, k, s).wait_send()
 
     @pl.loop(0, ny)
@@ -400,18 +409,33 @@
             for i in range(1, nx):
                 cross_copy(which, k, i).wait_send()
 
-    for s in range(2):
-        for which in range(2):
-            total = chunk[which, own_piece, starts[s] : starts[s + 1]]
+    for s in range(subs):
+        for which in range(2):
+            total = chunk[which, s, own_piece, :]
             for i in range(1, nx):
                 x_copy(which, s, i).wait_recv()
-                total = total + x_recv[s][which, i - 1].astype(F32)
-            grad_out[which * piece : (which + 1) * piece, starts[s] : starts[s + 1]] = total
+                total = total + x_recv[which, s, i - 1].astype(F32)
+            grad_out[which * piece : (which + 1) * piece, s * SUB : (s + 1) * SUB] = total
             for i in range(1, nx):
                 x_copy(which, s, i).wait_send()
 
 
-def shards(nx, widths, cotangent, routes, gate_weight, down_weight, saved_pre):
+def hand_on(*refs):
+    count = (len(refs) - 2) // 3
+    source, target, held = refs[:count], refs[count : 2 * count], refs[2 * count : 3 * count]
+    arrive, leave = refs[3 * count :]
+    incoming = [pltpu.make_async_copy(source[i], held[i], arrive.at[i]) for i in range(count)]
+    outgoing = [pltpu.make_async_copy(held[i], target[i], leave.at[i]) for i in range(count)]
+    for copy in incoming:
+        copy.start()
+    for first, second in zip(incoming, outgoing):
+        first.wait()
+        second.start()
+    for copy in outgoing:
+        copy.wait()
+
+
+def shards(nx, cotangent, routes, gate_weight, down_weight, saved_pre):
     peers = lax.axis_size("exp")
     ny = lax.axis_size("rep") // nx
     tokens, model = cotangent.shape
@@ -425,9 +449,9 @@
     block = GROUP * msg
     vmem = pl.BlockSpec(memory_space=pltpu.VMEM)
     dma = pltpu.SemaphoreType.DMA
-    wa, wb, wc = widths
-    grad, pair, token = pl.pallas_call(
-        functools.partial(kernel, ny, nx, peers, widths),
+    subs = (width - CROSS) // SUB
+    results = pl.pallas_call(
+        functools.partial(kernel, ny, nx, peers),
         out_shape=(
             jax.ShapeDtypeStruct((2 * piece, width), F32),
             jax.ShapeDtypeStruct((slots, double), BF),
@@ -454,21 +478,19 @@
             pltpu.VMEM((slots, 128), F32),
             pltpu.VMEM((slots, width), BF),
             pltpu.VMEM((slots, width), F32),
-            pltpu.VMEM((2, last, half, wa), BF),
-            pltpu.VMEM((2, last, half, wa), BF),
-            pltpu.VMEM((2, last, half, wb), BF),
-            pltpu.VMEM((2, last, half, wb), BF),
-            pltpu.VMEM((2, half, wa + wb), F32),
-            pltpu.VMEM((2, half, wa), BF),
-            pltpu.VMEM((2, nx - 1, piece, wa), BF),
-            pltpu.VMEM((2, half, wb), BF),
-            pltpu.VMEM((2, nx - 1, piece, wb), BF),
-            pltpu.VMEM((2, ny, half, wc), BF),
-            pltpu.VMEM((2, ny, nx - 1, piece, wc), BF),
-            pltpu.VMEM((2, last, piece, wc), BF),
-            pltpu.VMEM((2, last, piece, wc), BF),
+            pltpu.VMEM((2, ny, half, width - CROSS), F32),
+            pltpu.VMEM((2, last, subs, half, SUB), BF),
+            pltpu.VMEM((2, last, subs, half, SUB), BF),
+            pltpu.VMEM((2, subs, half, SUB), F32),
+            pltpu.VMEM((2, subs, half, SUB), BF),
+            pltpu.VMEM((2, subs, nx - 1, piece, SUB), BF),
+            pltpu.VMEM((2, ny, half, CROSS), BF),
+            pltpu.VMEM((2, ny, nx - 1, piece, CROSS), BF),
+            pltpu.VMEM((2, last, piece, CROSS), BF),
+            pltpu.VMEM((2, ny, piece, CROSS), BF),
             dma, dma((pairs,)), dma((pairs,)), dma((2,)), dma((2,)), dma, dma,
-            dma((2, last, 2)), dma((2, last, 2)), dma((2, 2, nx - 1)), dma((2, 2, nx - 1)),
+            dma((2, last, subs)), dma((2, last, subs)),
+            dma((2, subs, nx - 1)), dma((2, subs, nx - 1)),
             dma((2, ny, nx - 1)), dma((2, ny, nx - 1)), dma((2, last)), dma((2, last)),
         ],
         compiler_params=pltpu.CompilerParams(
@@ -485,6 +507,15 @@
         down_weight[0],
         saved_pre[0, 0],
     )
+    place = pl.BlockSpec(memory_space=pl.ANY)
+    grad, pair, token = pl.pallas_call(
+        hand_on,
+        out_shape=tuple(jax.ShapeDtypeStruct(r.shape, r.dtype) for r in results),
+        in_specs=[place] * 3,
+        out_specs=(place,) * 3,
+        scratch_shapes=[pltpu.VMEM(r.shape, r.dtype) for r in results] + [dma((3,)), dma((3,))],
+        name="results",
+    )(*results)
     return grad[None], pair[None, None], token.reshape(tokens, 1)
 
 
@@ -499,6 +530,6 @@
     )
     out_specs = (P("exp", "rep", None), P("rep", "exp", None, None), P(("rep", "exp"), None))
     return jax.shard_map(
-        functools.partial(shards, nx, WIDTHS), mesh=mesh, in_specs=in_specs, out_specs=out_specs,
+        functools.partial(shards, nx), mesh=mesh, in_specs=in_specs, out_specs=out_specs,
         check_vma=False,
     )

time: 120 us -> 111 us (0.925)
  local copies, waits for them, and re-layouts: 4.77 us -> 0 us
  Pallas kernels: 114 us -> 111 us
    unnamed x3 -> x0, local copies, waits for them, and re-layouts: 4.77 us -> none
    pallas_call x1 -> x2, Pallas kernels: 114 us -> 111 us  [the longest x1 109 us: shards(): pl.pallas_call(functools.partial(kernel, ny, nx, peers), out_shape=(jax.S...]
where the time goes in v3:
time: 111 us
  Pallas kernels  111 us (100%)
    pallas_call x1, Pallas kernels, shards(): pl.pallas_call(functools.partial(kernel, ny, nx, peers), out_shape=(jax.S...  109 us

profile of v3, /device:TPU:1, one launch (start us, length us, event | category | flops | bytes accessed | tf_op | source)
XLA Modules:
  0.0 111.2 jit_solution(2382294615307556346)
XLA Ops:
  0.6 108.6 %expert_backward.1 = (f32[128,768]{1,0:T(8,128)}, bf16[192,1536]{1,0:T(8,128)(2,1)}, f32[1,128]{1,0:T(1,128)}) custom-call(bf16[128,4096]{1,0:T(8,128)(2,1)} %cot.1, s32[1,128]{1,0:T(1,128)} %bitcast.11, f32[1,128]{1,0:T(1,128)} %bitcast.12, bf16[4096,768]{1,0:T(8,128)(2,1)} %bitcast.7, bf16[192,1536]{1,0:T(8,128)(2,1)} %bitcast.8), custom_call_target="tpu_custom_call" | custom-call | flops 2415919104 | bytes 12582912 | tf_op jit(solution)/shard_map/expert_backward/pallas_call | solution.py:453
  109.2 2.1 %results.1 = (f32[128,768]{1,0:T(8,128)}, bf16[192,1536]{1,0:T(8,128)(2,1)}, f32[1,128]{1,0:T(1,128)}) custom-call(f32[128,768]{1,0:T(8,128)} %get-tuple-element.9.refs_0_, bf16[192,1536]{1,0:T(8,128)(2,1)} %get-tuple-element.10.refs_1_, f32[1,128]{1,0:T(1,128)} %get-tuple-element.11.refs_2_), custom_call_target="tpu_custom_call" | custom-call | tf_op jit(solution)/shard_map/results/pallas_call | solution.py:511
